TPU v7x, 256 devices: a whole 4x4x8 slice. The times are simulated.
256 devices in a mesh: section: 2 (over core), wide: 16 (over x, z_lo), narrow: 8 (over y, z_hi).
Axes of the slice: x: 4, y: 4, z: 8 (z_hi: 2, z_lo: 4; z = z_hi * 4 + z_lo), core: 2. Of those that a mesh axis runs over, the one named last changes fastest.
Arguments:
- queries: bfloat16 [8, 1024, 8192], P('narrow', None, 'wide'), may hold values from -8 to 8
- keys_values: bfloat16 [8, 1024, 2048], P('narrow', None, 'wide'), may hold values from -6 to 6
- segments: int32 [8, 1024], P('narrow'), may hold values from 0 to 1016, as said below
- residual: bfloat16 [8, 1024, 8192], P('narrow', None, 'wide'), may hold values from -10 to 10
- out_weight: bfloat16 [8192, 8192], P('wide'), may hold values from -1 to 1
- key_weight: bfloat16 [8192, 512], P('wide'), may hold values from -0.0625 to 0.0625
- key_bias: float32 [512], replicated, may hold values from -4 to 4
- norm_gain: float32 [8192], P('wide'), may hold values from 0.5 to 1.5
Outputs:
- handed: bfloat16 [8, 1024, 8192], P('narrow', None, 'wide')
- keys_b: bfloat16 [8, 1024, 512], P('narrow', 'section')
Inputs may be any that keep to these rules, and one draw needn't show every extreme that they name: segments[s, t] is 0 at t = 0, never falls, changes only at multiples of 8, equals t wherever it changes, and the last 8 positions of every sequence form a text of their own.
All inputs are finite; a program needn't handle non-finite values.
Results may differ from a plain program's by a relative error of at most 0.025.
Values may be sent and summed in bfloat16 or wider, within the bound.
A program may use at most 128 MiB of HBM per device.

v0:
```python
import math

import jax
import jax.numpy as jnp
from jax import lax
from jax.sharding import PartitionSpec as P

D = 8192
HEAD = 128


theta = 1000000.0
eps = 1e-06
masked = -1e30


def swapped(block, axis, apart):
    count = lax.axis_size(axis)
    route = []
    for low in range(count):
        high = low | 1 << apart
        if high != low and high < count:
            route += [(low, high), (high, low)]
    return lax.ppermute(block, axis, route)


def shifted(x, axis, by):
    length = lax.axis_size(axis)
    pairs = [(i, i + by) for i in range(length) if 0 <= i + by < length]
    return lax.ppermute(x, axis, pairs)


def rotate(vectors, positions):
    half = HEAD // 2
    freq = jnp.power(theta, -2.0 * jnp.arange(half, dtype=jnp.float32) / HEAD)
    angles = positions.astype(jnp.float32)[:, None] * freq[None, :]
    cosine = jnp.cos(angles)[:, None, :]
    sine = jnp.sin(angles)[:, None, :]
    leading = vectors[..., :half]
    trailing = vectors[..., half:]
    return jnp.concatenate(
        [leading * cosine - trailing * sine, trailing * cosine + leading * sine], axis=-1
    )


def attend(query_rows, key_rows, value_rows, segments):
    length = query_rows.shape[0]
    groups = query_rows.shape[1] // HEAD
    block = min(length, 256)
    scale = 1.0 / math.sqrt(HEAD)
    positions = jnp.arange(length, dtype=jnp.int32)

    def one_block(index):
        offset = index * block
        picked = lax.dynamic_slice_in_dim(query_rows, offset, block, 0).reshape(
            block * groups, HEAD
        )
        scores = (
            lax.dot_general(
                picked, key_rows, (((1,), (1,)), ((), ())), preferred_element_type=jnp.float32
            )
            * scale
        )
        row_positions = offset + jnp.arange(block * groups, dtype=jnp.int32) // groups
        row_segments = jnp.repeat(lax.dynamic_slice_in_dim(segments, offset, block, 0), groups)
        allowed = (row_segments[:, None] == segments[None, :]) & (
            row_positions[:, None] >= positions[None, :]
        )
        scores = jnp.where(allowed, scores, masked)
        weights = jnp.exp(scores - jnp.max(scores, axis=-1, keepdims=True))
        probs = (weights / jnp.sum(weights, axis=-1, keepdims=True)).astype(jnp.bfloat16)
        context = jnp.dot(probs, value_rows, preferred_element_type=jnp.float32).astype(
            jnp.bfloat16
        )
        return context.reshape(block, groups * HEAD)

    blocks = lax.map(one_block, jnp.arange(length // block, dtype=jnp.int32))
    return blocks.reshape(length, groups * HEAD)


def local(queries, keys_values, segments, residual, out_weight, key_weight, key_bias, norm_gain):
    section_index = lax.axis_index("section")
    wide_index = lax.axis_index("wide")
    leading_section = section_index == 0
    query_rows = queries[0]
    pairs = keys_values[0]
    text_starts = segments[0]
    length = query_rows.shape[0]
    width = out_weight.shape[1]
    partner = swapped(pairs, "wide", 0)
    even = wide_index % 2 == 0
    key_rows = jnp.where(even, pairs, partner)
    value_rows = jnp.where(even, partner, pairs)
    context = lax.cond(
        leading_section,
        lambda: attend(query_rows, key_rows, value_rows, text_starts),
        lambda: jnp.zeros(query_rows.shape, jnp.bfloat16),
    )
    partial_value = lax.cond(
        leading_section,
        lambda: jnp.dot(context, out_weight, preferred_element_type=jnp.float32),
        lambda: jnp.zeros((length, width), jnp.float32),
    )
    summed = lax.psum_scatter(
        partial_value.astype(jnp.bfloat16), "wide", scatter_dimension=1, tiled=True
    ).astype(jnp.float32)
    produced = (residual[0].astype(jnp.float32) + summed).astype(jnp.bfloat16)
    arrived = shifted(produced, "section", 1)
    handed = jnp.where(leading_section, produced, arrived)
    half_len = length // 2
    first_row = section_index * half_len
    own_rows = lax.dynamic_slice_in_dim(handed, first_row, half_len, 0)
    hidden = own_rows.astype(jnp.float32)
    squares = lax.psum(jnp.sum(hidden * hidden, axis=-1), "wide")
    inverse = lax.rsqrt(squares / D + eps)
    normed = (hidden * inverse[:, None] * norm_gain).astype(jnp.bfloat16)
    key_cols = key_weight.shape[1]
    local_keys = jnp.dot(normed, key_weight, preferred_element_type=jnp.float32)
    projected = lax.psum(local_keys.astype(jnp.bfloat16), "wide").astype(jnp.float32) + key_bias
    positions = first_row + jnp.arange(half_len, dtype=jnp.int32)
    rotated = rotate(projected.reshape(half_len, key_cols // HEAD, HEAD), positions)
    keys_out = rotated.reshape(half_len, key_cols).astype(jnp.bfloat16)
    return (handed[None], keys_out[None])


def solution(mesh):
    return jax.shard_map(
        local,
        mesh=mesh,
        in_specs=(
            P("narrow", None, "wide"),
            P("narrow", None, "wide"),
            P("narrow", None),
            P("narrow", None, "wide"),
            P("wide", None),
            P("wide", None),
            P(),
            P("wide"),
        ),
        out_specs=(P("narrow", None, "wide"), P("narrow", "section", None)),
        check_vma=False,
    )
```

profile of v0, /device:TPU:8, one launch (start us, length us, event | category | flops | bytes accessed | tf_op | source)
XLA Modules:
  0.0 640.0 jit_solution(5216325618537207003)
XLA Ops:
  7.2 2.0 collective-permute-start
  9.2 6.5 %collective-permute-done = bf16[1024,128]{1,0:T(8,128)(2,1)S(1)} collective-permute-done((bf16[1024,128]{1,0:T(8,128)(2,1)}, bf16[1024,128]{1,0:T(8,128)(2,1)S(1)}, u32[]{:S(2)}, u32[]{:S(2)}) %collective-permute-start) | collective-permute-done | bytes 262176 | tf_op jit(solution)/shard_map/ppermute | solution.py:24
  15.7 31.1 %conditional.2 = (bf16[1024,512]{1,0:T(8,128)(2,1)}) conditional(s32[]{:T(128)} %convert_element_type.63, () %tuple.37, (bf16[1,1024,512]{2,1,0:T(8,128)(2,1)}, s32[]{:T(128)}, bf16[1024,128]{1,0:T(8,128)(2,1)}, bf16[1024,128]{1,0:T(8,128)(2,1)S(1)}, s32[1,1024]{1,0:T(1,128)}, /*index=5*/s32[]{:T(128)}, s32[]{:T(128)}, s32[]{:T(128)}, ...), branch_computations={%region_0.1_spmd, %region_1.6_spmd.clone} | conditional | flops 548805632 | bytes 16830324 | solution.py:94
  15.7 1.0 broadcast_select_fusion
  16.8 30.1 %while.15 = (s32[]{:T(128)}, bf16[4,256,512]{2,1,0:T(8,128)(2,1)}, s32[4]{0:T(128)S(1)}, s32[1024]{0:T(1024)}, s32[1,1024]{1,0:T(1,128)}, /*index=5*/bf16[1024,5...) while((s32[]{:T(128)}, bf16[4,256,512]{2,1,0:T(8,128)(2,1)}, ...), condition=%wide.region_5.5_spmd.clone, body=%wide.region_2.4_spmd.clone.sunk | while | flops 548543488 | bytes 15781563 | solution.py:77
  16.8 0.6 dynamic_slice.36
  17.9 1.0 constant_dynamic-slice_fusion.2
  18.9 0.2 reshape.119
  19.1 0.8 dynamic_slice.37
  19.9 0.1 eq.53
  20.1 1.8 fusion.38
  21.9 0.6 fusion.39
  22.5 0.9 fusion.40
  23.4 0.2 broadcast_in_dim.43
  23.6 0.7 constant_dynamic-update-slice_fusion.2
  24.3 0.6 dynamic_slice.36
  25.4 1.0 constant_dynamic-slice_fusion.2
  26.4 0.2 reshape.119
  26.6 0.8 dynamic_slice.37
  27.4 0.1 broadcast_in_dim.42
  27.5 0.1 eq.53
  27.6 1.8 fusion.38
  29.4 0.6 fusion.39
  30.0 0.9 fusion.40
  30.9 0.2 broadcast_in_dim.43
  31.1 0.7 constant_dynamic-update-slice_fusion.2
  31.8 0.6 dynamic_slice.36
  33.0 1.0 constant_dynamic-slice_fusion.2
  33.9 0.2 reshape.119
  34.1 0.8 dynamic_slice.37
  34.9 0.1 broadcast_in_dim.42
  35.0 0.1 eq.53
  35.1 1.8 fusion.38
  36.9 0.6 fusion.39
  37.5 0.9 fusion.40
  38.4 0.2 broadcast_in_dim.43
  38.6 0.7 constant_dynamic-update-slice_fusion.2
  39.3 0.6 dynamic_slice.36
  40.5 1.0 constant_dynamic-slice_fusion.2
  41.5 0.2 reshape.119
  41.6 0.8 dynamic_slice.37
  42.5 0.1 eq.53
  42.6 1.8 fusion.38
  44.4 0.6 fusion.39
  45.1 0.9 fusion.40
  46.0 0.2 broadcast_in_dim.43
  46.1 0.7 constant_dynamic-update-slice_fusion.2
  46.9 14.8 %conditional.3 = (bf16[1024,8192]{1,0:T(8,128)(2,1)}) conditional(s32[]{:T(128)} %convert_element_type.63, () %tuple.36, (bf16[1024,512]{1,0:T(8,128)(2,1)}, bf16[512,8192]{1,0:T(8,128)(2,1)}) %tuple.39), branch_computations={%region_6.7_spmd, %region_7.8_spmd} | conditional | flops 8589934592 | bytes 26214408 | solution.py:99
  46.9 14.8 %fusion.20 = bf16[1024,8192]{1,0:T(8,128)(2,1)} fusion(bf16[1024,512]{1,0:T(8,128)(2,1)} %get-tuple-element.162, bf16[512,8192]{1,0:T(8,128)(2,1)} %get-tuple-element.184), kind=kOutput, calls=%fused_computation.44 | convolution fusion | flops 8589934592 | bytes 26214400 | tf_op jit(solution)/shard_map/cond/branch_1_fun/dot_general | solution.py:101
  61.7 358.5 %reduce-scatter.2.cloned.1.call-done = bf16[1024,512]{1,0:T(8,128)(2,1)} async-done(((bf16[1024,8192]{1,0:T(8,128)(2,1)}), bf16[1024,512]{1,0:T(8,128)(2,1)}) %reduce-scatter.2.cloned.1.call-update) | async-done | bytes 1048592 | tf_op jit(solution)/shard_map/reduce_scatter | solution.py:104
  420.2 1.5 fusion.10
  421.7 2.5 collective-permute-start.1
  424.2 1.4 collective-permute-done.1
  425.7 0.1 broadcast_select_fusion.2
  425.8 0.2 fusion.11
  426.0 41.2 %psum.14 = f32[512]{0:T(512)S(1)} all-reduce(f32[512]{0:T(512)S(1)} %fusion.11), channel_id=1, replica_groups=mesh['section'=2,'wide'=16,'narrow'=8] {'wide'}, use_global_device_ids=true, to_apply=%region_10.11 | all-reduce | flops 512 | bytes 4096 | tf_op jit(solution)/shard_map/psum | solution.py:114
  467.2 1.3 convolution_convert_fusion
  468.6 1.0 multiply_cosine_fusion
  469.6 159.5 %all-reduce.2.cloned.1.call-done = bf16[512,512]{1,0:T(8,128)(2,1)} async-done(((bf16[512,512]{1,0:T(8,128)(2,1)}), bf16[512,512]{1,0:T(8,128)(2,1)}) %all-reduce.2.cloned.1.call-update) | async-done | bytes 524304 | tf_op jit(solution)/shard_map/psum | solution.py:119
  629.0 1.2 convert_add_fusion.1
  630.2 0.4 reshape.114
  630.6 0.9 subtract_convert_fusion
  631.4 0.7 pad_maximum_fusion
  632.2 1.0 convert_element_type.72
  (25 shorter events, 0.4 us)
Async XLA Ops:
  7.2 460.1 %copy-start = (bf16[512,512]{1,0:T(8,128)(2,1)S(1)}, bf16[512,512]{1,0:T(8,128)(2,1)}, u32[]{:S(2)}) copy-start(bf16[512,512]{1,0:T(8,128)(2,1)} %param.19) | copy-start | bytes 1572868
  7.2 413.0 %reduce-scatter.2.cloned.1.call-start = ((), (), s32[]{:S(2)}) async-start(), calls=%async_computation.1 | async-start | bytes 17825792 | tf_op jit(solution)/shard_map/reduce_scatter | solution.py:104
  7.2 8.5 %collective-permute-start = (bf16[1024,128]{1,0:T(8,128)(2,1)}, bf16[1024,128]{1,0:T(8,128)(2,1)S(1)}, u32[]{:S(2)}, u32[]{:S(2)}) collective-permute-start(bf16[1024,128]{1,0:T(8,128)(2,1)} %bitcast.28), channel_id=1, source_target_pairs={{0,8},{8,0},{16,24},{24,16},{32,40},{40,32},{48,56},{56,48},{64,72... | collective-permute-start | bytes 786440 | tf_op jit(solution)/shard_map/ppermute | solution.py:24
  61.6 358.6 %copy-start.2 = (bf16[1,1024,512]{2,1,0:T(8,128)(2,1)S(1)}, bf16[1,1024,512]{2,1,0:T(8,128)(2,1)}, u32[]{:S(2)}) copy-start(bf16[1,1024,512]{2,1,0:T(8,128)(2,1)} %param.17) | copy-start | bytes 3145732
  61.7 405.6 %copy-start.4 = (f32[512]{0:T(512)S(1)}, f32[512]{0:T(512)}, u32[]{:S(2)}) copy-start(f32[512]{0:T(512)} %param.21) | copy-start | bytes 6148
  61.7 567.4 %copy-start.3 = (f32[512]{0:T(512)S(1)}, f32[512]{0:T(512)}, u32[]{:S(2)}) copy-start(f32[512]{0:T(512)} %param.20) | copy-start | bytes 6148
  61.7 567.4 %all-reduce.2.cloned.1.call-start = ((), (), s32[]{:S(2)}) async-start(), calls=%async_computation.2 | async-start | bytes 1048576 | tf_op jit(solution)/shard_map/psum | solution.py:119
  421.7 4.0 collective-permute-start.1
  425.8 43.8 %copy-start.1 = (bf16[1024,512]{1,0:T(8,128)(2,1)}, bf16[1024,512]{1,0:T(8,128)(2,1)S(1)}, u32[]{:S(2)}) copy-start(bf16[1024,512]{1,0:T(8,128)(2,1)S(1)} %broadcast_select_fusion.2) | copy-start | bytes 3145732
Sparse Core Ops, SparseCore 0:
  61.8 358.3 reduce-scatter.1
  468.7 160.3 all-reduce.1
where the time goes:
time: 641 us; the launch traced here: 640 us
  waiting for transfers between devices  526 us (82%)
  blocking collectives  41.2 us (6%)
  matrix products  26.8 us (4%)
  local copies, waits for them, and re-layouts  15.7 us (2%)
  between operations  14.1 us (2%)
  other arithmetic  9.05 us (1%)
    reduce_scatter x1, waiting for transfers between devices, local(): lax.psum_scatter(partial_value.astype(jnp.bfloat16), 'wide', scatter_dime...  358 us
    psum x1, waiting for transfers between devices, local(): lax.psum(local_keys.astype(jnp.bfloat16), 'wide').astype(jnp.float32)  159 us
    psum x1, blocking collectives, local(): squares = lax.psum(jnp.sum(hidden * hidden, axis=-1), 'wide')  41.2 us
    dot_general x1, matrix products, local(): jnp.dot(context, out_weight, preferred_element_type=jnp.float32)  14.8 us
  transfers between devices with their start and end apart: 4, of which 4 were waited for; matrix products, arithmetic and copies ran while one was open for 0% of the time, Pallas kernels for 0%

commit v1 on v0

v1 whole, which is shorter than its diff:
```python
import functools
import math

import jax
import jax.numpy as jnp
import numpy as np
from jax import lax
from jax.experimental import pallas as pl
from jax.experimental.pallas import tpu as pltpu
from jax.sharding import PartitionSpec as P

MESH = pl.DeviceIdType.MESH
D = 8192
HEAD = 128
LEN = 1024
HALF = LEN // 2
COLS = 512
KEYS = 512
THETA = 1000000.0
EPS = 1e-06
MASKED = -1e30
SCALE = math.log2(math.e) / math.sqrt(HEAD)
BF16 = jnp.bfloat16
F32 = jnp.float32
WIDE_KEYS = KEYS + 128


def dot(a, b, dims=((1,), (0,))):
    return lax.dot_general(a, b, (dims, ((), ())), preferred_element_type=F32)


def split_sum(total):
    rows = total.shape[0]
    high = total.astype(BF16).astype(F32)
    low = total - high
    lane = lax.broadcasted_iota(jnp.int32, (rows, 128), 1)
    return jnp.where(lane < 64, high, low).astype(BF16)


def kernel(
    q_hbm, kv_hbm, seg_ref, res_hbm, w_hbm, kw_hbm, bias_ref, gain_ref, rot_hbm,
    hand_hbm, keys_hbm,
    qbuf, kvb, wbuf, resb, kwb, rotb, cbuf, pbuf, xsend, xrecv, zsend, zrecv, hbuf,
    k1s, k1r, k2s, k2r, k3,
    l_sem, wl_sem, kv_sem, wx_sem, wy_sem, c_sem, p_sem, zs_sem, zr_sem, h_sem, hl_sem,
    ks_sem, kr_sem, kl_sem,
):
    c = lax.axis_index("section")
    w = lax.axis_index("wide")
    n = lax.axis_index("narrow")
    x, z = w // 4, w % 4
    y, h = n // 2, n % 2

    def at(c_=None, x_=None, y_=None, z_=None):
        xx = x if x_ is None else x_
        zz = z if z_ is None else z_
        yy = y if y_ is None else y_
        return {"section": c if c_ is None else c_, "wide": xx * 4 + zz, "narrow": yy * 2 + h}

    def plus(value, by):
        return (value + by) % 4

    started = []

    def send(src, dst, send_sem, recv_sem, to):
        copy = pltpu.make_async_remote_copy(
            src_ref=src, dst_ref=dst, send_sem=send_sem, recv_sem=recv_sem,
            device_id=to, device_id_type=MESH,
        )
        copy.start()
        started.append(copy)

    def arrived(dst, recv_sem):
        pltpu.make_async_remote_copy(
            src_ref=dst, dst_ref=dst, send_sem=recv_sem, recv_sem=recv_sem,
            device_id=at(1 - c), device_id_type=MESH,
        ).wait_recv()

    owner = [3 * (1 - z // 2), (2 + 3 * z) % 5, 1 + z % 2, z]
    pair = z + 1 - 2 * (z % 2)
    mine = z % 2
    rows = pl.ds(pl.multiple_of(c * HALF, HALF), HALF)

    heads = pl.ds(pl.multiple_of(c * 256, 256), 256)
    local_kv = pltpu.make_async_copy(kv_hbm, kvb.at[mine], l_sem.at[0])
    local_q = pltpu.make_async_copy(q_hbm.at[:, heads], qbuf, l_sem.at[1])
    local_res = pltpu.make_async_copy(res_hbm.at[rows], resb, l_sem.at[2])
    local_kw = pltpu.make_async_copy(kw_hbm, kwb, l_sem.at[3])
    local_rot = [
        pltpu.make_async_copy(
            rot_hbm.at[:, pl.ds(pl.multiple_of(c * HALF + 256 * g + 64 * x + 16 * z, 16), 16)],
            rotb.at[g], l_sem.at[4 + g],
        )
        for g in range(2)
    ]

    def columns(k, x_):
        return pl.ds(pl.multiple_of(x_ * (4 * COLS) + owner[k] * COLS, COLS), COLS)

    local_w = [
        pltpu.make_async_copy(w_hbm.at[heads, columns(k, x)], wbuf.at[k, 0], wl_sem.at[k])
        for k in range(4)
    ]
    for copy in [local_kv, local_q, *local_w, local_res, local_kw, *local_rot]:
        copy.start()

    barrier = pltpu.get_barrier_semaphore()
    partners = [at(1 - c)]
    for d in range(1, 4):
        partners += [at(x_=plus(x, d)), at(y_=plus(y, d)), at(z_=plus(z, d))]
    for to in partners:
        pl.semaphore_signal(barrier, inc=1, device_id=to, device_id_type=MESH)
    pl.semaphore_wait(barrier, len(partners))

    send(kv_hbm.at[rows], kvb.at[mine, rows], kv_sem.at[0], kv_sem.at[1], at(z_=pair))
    part = pl.ds(pl.multiple_of(y * 64, 64), 64)
    w_rows = pl.ds(pl.multiple_of(c * 256 + y * 64, 64), 64)
    for k in range(4):
        for d in range(1, 4):
            to = plus(x, 4 - d)
            send(w_hbm.at[w_rows, columns(k, to)], wbuf.at[k, d, part],
                 wx_sem.at[0, k, d], wx_sem.at[1, k, d], at(x_=to))

    def share_weights(k):
        for d in range(1, 4):
            arrived(wbuf.at[k, d, part], wx_sem.at[1, k, d])
        for e in range(1, 4):
            send(wbuf.at[k, pl.ds(1, 3), part], wbuf.at[k, pl.ds(1, 3), part],
                 wy_sem.at[0, k, e], wy_sem.at[1, k, e], at(y_=plus(y, e)))

    def await_weights(k):
        local_w[k].wait()
        for e in range(1, 4):
            theirs = pl.ds(pl.multiple_of(plus(y, 4 - e) * 64, 64), 64)
            arrived(wbuf.at[k, pl.ds(1, 3), theirs], wy_sem.at[1, k, e])

    local_kv.wait()
    local_q.wait()
    arrived(kvb.at[1 - mine, rows], kv_sem.at[1])
    send(kvb.at[1 - mine, rows], kvb.at[1 - mine, rows], kv_sem.at[2], kv_sem.at[3], at(1 - c))
    share_weights(0)
    other_rows = pl.ds(pl.multiple_of((1 - c) * HALF, HALF), HALF)
    arrived(kvb.at[1 - mine, other_rows], kv_sem.at[3])

    def attend(index):
        seen = 128 * (index + 1)
        here = pl.ds(128 * index, 128)
        picked = jnp.concatenate([qbuf[here, :HEAD], qbuf[here, HEAD:]], axis=0)
        scores = dot(kvb[0, :seen, :], picked, ((1,), (1,)))
        first = seg_ref[:, here]
        first = jnp.concatenate([first, first], axis=1)
        key_at = lax.broadcasted_iota(jnp.int32, (seen, 256), 0)
        query_at = 128 * index + lax.broadcasted_iota(jnp.int32, (seen, 256), 1) % 128
        scores = jnp.where((key_at >= first) & (key_at <= query_at), scores, MASKED)
        top = jnp.max(scores, axis=0, keepdims=True)
        weights = jnp.exp2((scores - top) * SCALE)
        total = jnp.sum(weights, axis=0, keepdims=True)
        context = dot(kvb[1, :seen, :], weights.astype(BF16), ((0,), (0,)))
        return (context / total).T.astype(BF16)

    def context_block(b):
        for half in range(2):
            context = attend(b + 4 * half)
            there = pl.ds(128 * half, 128)
            cbuf[0, b, there, :HEAD] = context[:128]
            cbuf[0, b, there, HEAD:] = context[128:]
        for d in range(1, 4):
            send(cbuf.at[0, b], cbuf.at[d, b], c_sem.at[0, b, d], c_sem.at[1, b, d],
                 at(x_=plus(x, 4 - d)))

    for b in range(4):
        context_block(b)
        if b < 3:
            share_weights(b + 1)

    units = [(k, 2 * g + j) for g in range(2) for k in range(4) for j in range(2)]
    met_k, met_b = set(), set()

    def multiply(u):
        k, b = units[u]
        if k not in met_k:
            met_k.add(k)
            await_weights(k)
        if b not in met_b:
            met_b.add(b)
            for d in range(1, 4):
                arrived(cbuf.at[d, b], c_sem.at[1, b, d])
        total = dot(cbuf[0, b], wbuf[k, 0])
        for d in range(1, 4):
            total += dot(cbuf[d, b], wbuf[k, d])
        slot = u % 2
        pbuf[slot, 0] = total[:128]
        pbuf[slot, 1] = total[128:]
        xsend[u] = pbuf[slot, 1 - c].astype(BF16)
        send(xsend.at[u], xrecv.at[u], p_sem.at[0, u], p_sem.at[1, u], at(1 - c))

    def pass_on(u):
        k, b = units[u]
        arrived(xrecv.at[u], p_sem.at[1, u])
        total = pbuf[u % 2, c] + xrecv[u].astype(F32)
        if k < 3:
            to = owner[k]
            up = to > z
            has = (up & (z > 0)) | (jnp.logical_not(up) & (z < 3))

            @pl.when(has)
            def _():
                arrived(zrecv.at[to, b], zr_sem.at[to, b])
                zsend[k, b] = (total + zrecv[to, b].astype(F32)).astype(BF16)

            @pl.when(jnp.logical_not(has))
            def _():
                zsend[k, b] = total.astype(BF16)

            following = jnp.where(up, z + 1, z - 1)
            slot = jnp.where(jnp.logical_not(up) & (to == following), 4, to)
            send(zsend.at[k, b], zrecv.at[slot, b], zs_sem.at[k, b], zr_sem.at[slot, b],
                 at(z_=following))
        else:
            pbuf[u % 2, c] = total + resb[pl.ds(128 * b, 128), :].astype(F32)

            @pl.when(z > 0)
            def _():
                arrived(zrecv.at[z, b], zr_sem.at[z, b])
                pbuf[u % 2, c] += zrecv[z, b].astype(F32)

            @pl.when(z < 3)
            def _():
                arrived(zrecv.at[4, b], zr_sem.at[4, b])
                pbuf[u % 2, c] += zrecv[4, b].astype(F32)

            hbuf[b] = pbuf[u % 2, c].astype(BF16)
            place = pl.ds(pl.multiple_of(c * HALF + 128 * b, 128), 128)
            local = pltpu.make_async_copy(hbuf.at[b], hand_hbm.at[place], hl_sem.at[b])
            local.start()
            locals_.append(local)
            send(hbuf.at[b], hand_hbm.at[place], h_sem.at[0, b], h_sem.at[1, b], at(1 - c))

    locals_ = []

    def keys_1(g):
        hidden = hbuf[pl.ds(2 * g, 2)].reshape(256, COLS).astype(F32)
        squares = jnp.sum(hidden * hidden, axis=1, keepdims=True)
        partial = dot((hidden * gain_ref[...]).astype(BF16), kwb[...])
        k1s[g, :, :KEYS] = partial.astype(BF16)
        k1s[g, :, KEYS:] = split_sum(squares)
        for d in range(1, 4):
            to = plus(x, 4 - d)
            send(k1s.at[g, pl.ds(pl.multiple_of(to * 64, 64), 64)], k1r.at[g, d],
                 ks_sem.at[0, g, d], kr_sem.at[0, g, d], at(x_=to))

    def keys_2(g):
        total = k1s[g, pl.ds(pl.multiple_of(x * 64, 64), 64), :].astype(F32)
        for d in range(1, 4):
            arrived(k1r.at[g, d], kr_sem.at[0, g, d])
            total += k1r[g, d].astype(F32)
        squares = total[:, KEYS : KEYS + 1] + total[:, KEYS + 64 : KEYS + 65]
        k2s[g, :, :KEYS] = total[:, :KEYS].astype(BF16)
        k2s[g, :, KEYS:] = split_sum(squares)
        for e in range(1, 4):
            to = plus(z, e)
            send(k2s.at[g, pl.ds(pl.multiple_of(to * 16, 16), 16)], k2r.at[g, e],
                 ks_sem.at[1, g, e], kr_sem.at[1, g, e], at(z_=to))

    def keys_3(g):
        at_rows = pl.ds(pl.multiple_of(z * 16, 16), 16)
        total = k2s[g, at_rows, :].astype(F32)
        for e in range(1, 4):
            arrived(k2r.at[g, e], kr_sem.at[1, g, e])
            total += k2r[g, e].astype(F32)
        squares = total[:, KEYS : KEYS + 1] + total[:, KEYS + 64 : KEYS + 65]
        projected = total[:, :KEYS] * lax.rsqrt(squares / D + EPS) + bias_ref[...]
        cosine, sine = rotb[g, 0], rotb[g, 1]
        for head in range(KEYS // HEAD):
            v = projected[:, head * HEAD : (head + 1) * HEAD]
            crossed = jnp.concatenate([v[:, HEAD // 2 :], v[:, : HEAD // 2]], axis=1)
            k3[g, at_rows, head * HEAD : (head + 1) * HEAD] = (v * cosine + crossed * sine).astype(BF16)
        for e in range(1, 4):
            send(k3.at[g, at_rows], k3.at[g, at_rows], ks_sem.at[2, g, e], kr_sem.at[2, g, e],
                 at(z_=plus(z, e)))

    def keys_4(g):
        for e in range(1, 4):
            theirs = pl.ds(pl.multiple_of(plus(z, 4 - e) * 16, 16), 16)
            arrived(k3.at[g, theirs], kr_sem.at[2, g, e])
        place = pl.ds(pl.multiple_of(256 * g + x * 64, 64), 64)
        local = pltpu.make_async_copy(k3.at[g], keys_hbm.at[place], kl_sem.at[g])
        local.start()
        locals_.append(local)
        for d in range(1, 4):
            send(k3.at[g], keys_hbm.at[place], ks_sem.at[3, g, d], kr_sem.at[3, g, d],
                 at(x_=plus(x, d)))

    local_res.wait()
    local_kw.wait()
    for copy in local_rot:
        copy.wait()
    last = len(units) - 1
    for u in range(last + 2):
        if u <= last:
            multiply(u)
        if u >= 1:
            pass_on(u - 1)
        if u == 8:
            keys_1(0)
        if u == 10:
            keys_2(0)
        if u == 12:
            keys_3(0)
        if u == 14:
            keys_4(0)
    keys_1(1)
    keys_2(1)
    keys_3(1)
    keys_4(1)
    for b in range(4):
        place = pl.ds(pl.multiple_of((1 - c) * HALF + 128 * b, 128), 128)
        arrived(hand_hbm.at[place], h_sem.at[1, b])
    for g in range(2):
        for d in range(1, 4):
            place = pl.ds(pl.multiple_of(256 * g + plus(x, 4 - d) * 64, 64), 64)
            arrived(keys_hbm.at[place], kr_sem.at[3, g, d])
    for copy in locals_:
        copy.wait()
    for copy in started:
        copy.wait_send()


def rotation():
    angles = np.arange(LEN)[:, None] * THETA ** (-2.0 * np.arange(HEAD // 2) / HEAD)[None, :]
    cosine, sine = np.cos(angles), np.sin(angles)
    return np.stack(
        [np.concatenate([cosine, cosine], 1), np.concatenate([-sine, sine], 1)]
    ).astype(np.float32)


def local(queries, keys_values, segments, residual, out_weight, key_weight, key_bias, norm_gain):
    hbm = pl.BlockSpec(memory_space=pl.ANY)
    vmem = pl.BlockSpec(memory_space=pltpu.VMEM)
    dma = pltpu.SemaphoreType.DMA
    handed, keys = pl.pallas_call(
        kernel,
        out_shape=(
            jax.ShapeDtypeStruct((LEN, COLS), BF16),
            jax.ShapeDtypeStruct((HALF, KEYS), BF16),
        ),
        in_specs=[hbm, hbm, vmem, hbm, hbm, hbm, vmem, vmem, hbm],
        out_specs=(hbm, hbm),
        scratch_shapes=[
            pltpu.VMEM((LEN, 256), BF16),
            pltpu.VMEM((2, LEN, HEAD), BF16),
            pltpu.VMEM((4, 4, 256, COLS), BF16),
            pltpu.VMEM((HALF, COLS), BF16),
            pltpu.VMEM((COLS, KEYS), BF16),
            pltpu.VMEM((2, 2, 16, HEAD), F32),
            pltpu.VMEM((4, 4, 256, 256), BF16),
            pltpu.VMEM((2, 2, 128, COLS), F32),
            pltpu.VMEM((16, 128, COLS), BF16),
            pltpu.VMEM((16, 128, COLS), BF16),
            pltpu.VMEM((3, 4, 128, COLS), BF16),
            pltpu.VMEM((5, 4, 128, COLS), BF16),
            pltpu.VMEM((4, 128, COLS), BF16),
            pltpu.VMEM((2, 256, WIDE_KEYS), BF16),
            pltpu.VMEM((2, 4, 64, WIDE_KEYS), BF16),
            pltpu.VMEM((2, 64, WIDE_KEYS), BF16),
            pltpu.VMEM((2, 4, 16, WIDE_KEYS), BF16),
            pltpu.VMEM((2, 64, KEYS), BF16),
            dma((6,)),
            dma((4,)),
            dma((4,)),
            dma((2, 4, 4)),
            dma((2, 4, 4)),
            dma((2, 4, 4)),
            dma((2, 16)),
            dma((3, 4)),
            dma((5, 4)),
            dma((2, 4)),
            dma((4,)),
            dma((4, 2, 4)),
            dma((4, 2, 4)),
            dma((2,)),
        ],
        compiler_params=pltpu.CompilerParams(
            collective_id=0, has_side_effects=True, vmem_limit_bytes=56 << 20
        ),
        name="relay",
    )(
        queries[0], keys_values[0], segments, residual[0], out_weight, key_weight,
        key_bias.reshape(1, KEYS), norm_gain.reshape(1, COLS), jnp.asarray(rotation()),
    )
    return handed[None], keys[None]


def solution(mesh):
    return jax.shard_map(
        local,
        mesh=mesh,
        in_specs=(
            P("narrow", None, "wide"),
            P("narrow", None, "wide"),
            P("narrow", None),
            P("narrow", None, "wide"),
            P("wide", None),
            P("wide", None),
            P(),
            P("wide"),
        ),
        out_specs=(P("narrow", None, "wide"), P("narrow", "section", None)),
        check_vma=False,
    )
```

time: 641 us -> 99.5 us (0.16)
  waiting for transfers between devices: 526 us -> 0 us
  Pallas kernels: 0 us -> 94.2 us
  blocking collectives: 41.2 us -> 0 us
  matrix products: 26.8 us -> 0 us
  between operations: 14.1 us -> 0.64 us
  local copies, waits for them, and re-layouts: 15.7 us -> 4.13 us
  other arithmetic: 9.05 us -> 0 us
    reduce_scatter x1 -> x0, waiting for transfers between devices: 358 us -> none  [local(): lax.psum_scatter(partial_value.astype(jnp.bfloat16), 'wide', scatter_dime...]
    psum x1 -> x0, waiting for transfers between devices: 159 us -> none  [local(): lax.psum(local_keys.astype(jnp.bfloat16), 'wide').astype(jnp.float32)]
    pallas_call x0 -> x1, Pallas kernels: none -> 94.2 us  [local(): pl.pallas_call(kernel, out_shape=(jax.ShapeDtypeStruct((LEN, COLS), BF16)...]
    psum x1 -> x0, blocking collectives: 41.2 us -> none  [local(): squares = lax.psum(jnp.sum(hidden * hidden, axis=-1), 'wide')]
    dot_general x10 -> x0, matrix products: 26.8 us -> none  [the longest x1 14.8 us: local(): jnp.dot(context, out_weight, preferred_element_type=jnp.float32)]
    dynamic_slice x12 -> x0, local copies, waits for them, and re-layouts: 9.26 us -> none  [the longest x4 3.89 us: one_block(): lax.dynamic_slice_in_dim(query_rows, offset, block, 0)]
    ppermute x2 -> x0, waiting for transfers between devices: 7.95 us -> none  [the longest x1 6.52 us: swapped(): return lax.ppermute(block, axis, route)]
  transfers between devices with their start and end apart: 4 -> 0, of which waited for: 4 -> 0; matrix products, arithmetic and copies ran while one was open for 0% -> 0% of each run, Pallas kernels for 0% -> 0%
where the time goes in v1:
time: 99.5 us; the launch traced here: 98.9 us
  Pallas kernels  94.2 us (95%)
  local copies, waits for them, and re-layouts  4.13 us (4%)
    pallas_call x1, Pallas kernels, local(): pl.pallas_call(kernel, out_shape=(jax.ShapeDtypeStruct((LEN, COLS), BF16)...  94.2 us
    unnamed x2, local copies, waits for them, and re-layouts  4.13 us

profile of v1, /device:TPU:8, one launch (start us, length us, event | category | flops | bytes accessed | tf_op | source)
XLA Modules:
  0.0 98.9 jit_solution(11620195927520331716)
XLA Ops:
  0.6 94.2 %relay.1 = (bf16[1024,512]{1,0:T(8,128)(2,1)}, bf16[512,512]{1,0:T(8,128)(2,1)}) custom-call(bf16[1024,512]{1,0:T(8,128)(2,1)} %bitcast.8, bf16[1024,128]{1,0:T(8,128)(2,1)} %bitcast.11, s32[1,1024]{1,0:T(1,128)} %seg_ref.1, bf16[1024,512]{1,0:T(8,128)(2,1)} %bitcast.9, bf16[512,8192]{1,0:T(8,128)(2,1)} %w_hbm.1, bf16[512,512]{1,0:T(8,128)(2,1)} %kw_hbm.1, ...), custom_call_target="tpu_custom_call" | custom-call | tf_op jit(solution)/shard_map/relay/pallas_call | solution.py:341
  94.8 2.3 %copy.13 = bf16[1,1024,512]{2,1,0:T(8,128)(2,1)} copy(bf16[1,1024,512]{2,1,0:T(8,128)(2,1)} %bitcast.7) | data formatting | bytes 2097152
  97.1 1.9 %copy.14 = bf16[1,512,512]{2,1,0:T(8,128)(2,1)} copy(bf16[1,512,512]{2,1,0:T(8,128)(2,1)} %bitcast.10) | data formatting | bytes 1048576

commit v2 on v1

v2 whole, which is shorter than its diff:
```python
import functools
import math

import jax
import jax.numpy as jnp
import numpy as np
from jax import lax
from jax.experimental import pallas as pl
from jax.experimental.pallas import tpu as pltpu
from jax.sharding import PartitionSpec as P

MESH = pl.DeviceIdType.MESH
D = 8192
HEAD = 128
LEN = 1024
HALF = LEN // 2
COLS = 512
KEYS = 512
THETA = 1000000.0
EPS = 1e-06
MASKED = -1e30
SCALE = math.log2(math.e) / math.sqrt(HEAD)
BF16 = jnp.bfloat16
F32 = jnp.float32
GROUP = 256
UNITS = [(k, b) for k in range(4) for b in range(4)]


def dot(a, b, dims=((1,), (0,))):
    return lax.dot_general(a, b, (dims, ((), ())), preferred_element_type=F32)


def kernel(
    q_hbm, kv_hbm, seg_ref, res_hbm, w_hbm, kw_hbm, gain_ref,
    hand_hbm, keys_hbm, squares_ref,
    qbuf, kvb, wbuf, resb, kwb, gkb, cbuf, pbuf, xsend, xrecv, zsend, zrecv, hbuf,
    k1s, k1r, k2s, k2r, k3, sq1, sq2,
    l_sem, wl_sem, kv_sem, wx_sem, wy_sem, c_sem, p_sem, zs_sem, zr_sem, h_sem, hl_sem,
    gs_sem, gr_sem, ks_sem, kr_sem, kl_sem, qs_sem, qr_sem,
):
    c = lax.axis_index("section")
    w = lax.axis_index("wide")
    n = lax.axis_index("narrow")
    x, z = w // 4, w % 4
    y, h = n // 2, n % 2

    def at(c_=None, x_=None, y_=None, z_=None):
        xx = x if x_ is None else x_
        zz = z if z_ is None else z_
        yy = y if y_ is None else y_
        return {"section": c if c_ is None else c_, "wide": xx * 4 + zz, "narrow": yy * 2 + h}

    def plus(value, by):
        return (value + by) % 4

    started = []

    def send(src, dst, send_sem, recv_sem, to):
        copy = pltpu.make_async_remote_copy(
            src_ref=src, dst_ref=dst, send_sem=send_sem, recv_sem=recv_sem,
            device_id=to, device_id_type=MESH,
        )
        copy.start()
        started.append(copy)

    def arrived(dst, recv_sem):
        pltpu.make_async_remote_copy(
            src_ref=dst, dst_ref=dst, send_sem=recv_sem, recv_sem=recv_sem,
            device_id=at(1 - c), device_id_type=MESH,
        ).wait_recv()

    barrier = pltpu.get_barrier_semaphore()
    partners = [at(1 - c)]
    for d in range(1, 4):
        partners += [at(x_=plus(x, d)), at(y_=plus(y, d)), at(z_=plus(z, d))]
    for to in partners:
        pl.semaphore_signal(barrier, inc=1, device_id=to, device_id_type=MESH)

    owner = [3 * (1 - z // 2), (2 + 3 * z) % 5, 1 + z % 2, z]
    pair = z + 1 - 2 * (z % 2)
    mine = z % 2
    rows = pl.ds(pl.multiple_of(c * HALF, HALF), HALF)

    heads = pl.ds(pl.multiple_of(c * 256, 256), 256)
    local_kv = pltpu.make_async_copy(kv_hbm, kvb.at[mine], l_sem.at[0])
    local_q = pltpu.make_async_copy(q_hbm.at[:, heads], qbuf, l_sem.at[1])
    local_res = pltpu.make_async_copy(res_hbm.at[rows], resb, l_sem.at[2])
    local_kw = pltpu.make_async_copy(kw_hbm, kwb, l_sem.at[3])
    def columns(k, x_):
        return pl.ds(pl.multiple_of(x_ * (4 * COLS) + owner[k] * COLS, COLS), COLS)

    local_w = [
        pltpu.make_async_copy(w_hbm.at[heads, columns(k, x)], wbuf.at[k, 0], wl_sem.at[k])
        for k in range(4)
    ]
    for copy in [local_kv, local_kw, local_q, *local_w, local_res]:
        copy.start()

    pl.semaphore_wait(barrier, len(partners))

    send(kv_hbm.at[rows], kvb.at[mine, rows], kv_sem.at[0], kv_sem.at[1], at(z_=pair))
    part = pl.ds(pl.multiple_of(y * 64, 64), 64)
    w_rows = pl.ds(pl.multiple_of(c * 256 + y * 64, 64), 64)

    def send_weights(k):
        for d in range(1, 4):
            to = plus(x, 4 - d)
            send(w_hbm.at[w_rows, columns(k, to)], wbuf.at[k, d, part],
                 wx_sem.at[0, k, d], wx_sem.at[1, k, d], at(x_=to))

    def weights(i, e):
        theirs = pl.ds(pl.multiple_of(plus(y, 4 - e) * 64, 64), 64)
        return wbuf.at[i // 2, pl.ds(1, 3), theirs, pl.ds(256 * (i % 2), 256)]

    met_x = set()

    def share_weights(i):
        if i // 2 not in met_x:
            met_x.add(i // 2)
            for d in range(1, 4):
                arrived(wbuf.at[i // 2, d, part], wx_sem.at[1, i // 2, d])
        piece = weights(i, 0)
        for e in (1, 3):
            send(piece, piece, wy_sem.at[0, i, e], wy_sem.at[1, i, e], at(y_=plus(y, e)))

    ahead = 1 + 2 * c

    def pass_weights(i):
        piece = weights(i, ahead)
        arrived(piece, wy_sem.at[1, i, ahead])
        send(piece, piece, wy_sem.at[0, i, 2], wy_sem.at[1, i, 2], at(y_=plus(y, ahead)))

    def await_weights(k):
        local_w[k].wait()
        for i in (2 * k, 2 * k + 1):
            for e in (4 - ahead, 2):
                arrived(weights(i, e), wy_sem.at[1, i, e])

    def pass_context(b):
        arrived(cbuf.at[4 - ahead, b], c_sem.at[1, b, 4 - ahead])
        send(cbuf.at[4 - ahead, b], cbuf.at[2, b], c_sem.at[0, b, 2], c_sem.at[1, b, 2],
             at(x_=plus(x, ahead)))

    def pass_pair(_):
        arrived(kvb.at[1 - mine, rows], kv_sem.at[1])
        send(kvb.at[1 - mine, rows], kvb.at[1 - mine, rows], kv_sem.at[2], kv_sem.at[3], at(1 - c))

    def await_pair(_):
        local_kv.wait()
        local_q.wait()
        other_rows = pl.ds(pl.multiple_of((1 - c) * HALF, HALF), HALF)
        arrived(kvb.at[1 - mine, other_rows], kv_sem.at[3])

    def send_key_weights(_):
        local_kw.wait()
        gain = jnp.broadcast_to(gain_ref[...], (8, COLS)).T[:, :1]
        gkb[z] = (kwb[...].astype(F32) * gain).astype(BF16).reshape(2, 256, KEYS)
        for e in range(1, 4):
            send(gkb.at[z, c, part], gkb.at[z, c, part], gs_sem.at[0, e], gr_sem.at[0, e],
                 at(z_=plus(z, e)))

    def key_weights(e_y):
        theirs = pl.ds(pl.multiple_of(plus(y, 4 - e_y) * 64, 64), 64)
        return [gkb.at[plus(z, e), c, theirs] for e in range(1, 4)]

    def share_key_weights(_):
        for e in range(1, 4):
            arrived(gkb.at[plus(z, 4 - e), c, part], gr_sem.at[0, e])
        for e_y in (1, 3):
            for i, piece in enumerate(key_weights(0)):
                send(piece, piece, gs_sem.at[e_y, i], gr_sem.at[e_y, i], at(y_=plus(y, e_y)))

    def pass_key_weights(_):
        for i, piece in enumerate(key_weights(ahead)):
            arrived(piece, gr_sem.at[ahead, i])
            send(piece, piece, gs_sem.at[2, i], gr_sem.at[2, i], at(y_=plus(y, ahead)))

    def swap_key_weights(_):
        for e_y in (4 - ahead, 2):
            for i, piece in enumerate(key_weights(e_y)):
                arrived(piece, gr_sem.at[e_y, i])
        for e in range(1, 4):
            piece = gkb.at[plus(z, e), c]
            send(piece, piece, gs_sem.at[4, e], gr_sem.at[4, e], at(1 - c))

    def await_key_weights():
        for e in range(1, 4):
            arrived(gkb.at[plus(z, e), 1 - c], gr_sem.at[4, e])

    def attend(index):
        seen = 128 * (index + 1)
        here = pl.ds(128 * index, 128)
        picked = jnp.concatenate([qbuf[here, :HEAD], qbuf[here, HEAD:]], axis=0)
        scores = dot(kvb[0, :seen, :], picked, ((1,), (1,)))
        first = seg_ref[:, here]
        first = jnp.concatenate([first, first], axis=1)
        key_at = lax.broadcasted_iota(jnp.int32, (seen, 256), 0)
        query_at = 128 * index + lax.broadcasted_iota(jnp.int32, (seen, 256), 1) % 128
        scores = jnp.where((key_at >= first) & (key_at <= query_at), scores, MASKED)
        top = jnp.max(scores, axis=0, keepdims=True)
        weights = jnp.exp2((scores - top) * SCALE)
        total = jnp.sum(weights, axis=0, keepdims=True)
        context = dot(kvb[1, :seen, :], weights.astype(BF16), ((0,), (0,)))
        return (context / total).T.astype(BF16)

    def context_block(b):
        for half in range(2):
            context = attend(b + 4 * half)
            there = pl.ds(128 * half, 128)
            cbuf[0, b, there, :HEAD] = context[:128]
            cbuf[0, b, there, HEAD:] = context[128:]
        for d in (1, 3):
            send(cbuf.at[0, b], cbuf.at[d, b], c_sem.at[0, b, d], c_sem.at[1, b, d],
                 at(x_=plus(x, 4 - d)))

    met_k, met_b = set(), set()

    def multiply(u):
        k, b = UNITS[u]
        if k not in met_k:
            met_k.add(k)
            await_weights(k)
        if b not in met_b:
            met_b.add(b)
            arrived(cbuf.at[ahead, b], c_sem.at[1, b, ahead])
            arrived(cbuf.at[2, b], c_sem.at[1, b, 2])
        total = dot(cbuf[0, b], wbuf[k, 0])
        for d in range(1, 4):
            total += dot(cbuf[d, b], wbuf[k, d])
        pbuf[u, 0] = total[:128]
        pbuf[u, 1] = total[128:]
        xsend[u] = pbuf[u, 1 - c].astype(BF16)
        send(xsend.at[u], xrecv.at[u], p_sem.at[0, u], p_sem.at[1, u], at(1 - c))

    def add_half(u):
        k, b = UNITS[u]
        arrived(xrecv.at[u], p_sem.at[1, u])
        total = pbuf[u, c] + xrecv[u].astype(F32)
        if k == 3:
            total += resb[pl.ds(128 * b, 128), :].astype(F32)
        pbuf[u, c] = total

    def pass_on(u):
        k, b = UNITS[u]
        to = owner[k]
        up = to > z
        has = (up & (z > 0)) | (jnp.logical_not(up) & (z < 3))

        @pl.when(has)
        def _():
            arrived(zrecv.at[to, b], zr_sem.at[to, b])
            zsend[k, b] = (pbuf[u, c] + zrecv[to, b].astype(F32)).astype(BF16)

        @pl.when(jnp.logical_not(has))
        def _():
            zsend[k, b] = pbuf[u, c].astype(BF16)

        following = jnp.where(up, z + 1, z - 1)
        slot = jnp.where(jnp.logical_not(up) & (to == following), 4, to)
        send(zsend.at[k, b], zrecv.at[slot, b], zs_sem.at[k, b], zr_sem.at[slot, b],
             at(z_=following))

    locals_ = []

    def hand(b):
        u = UNITS.index((3, b))
        held = pbuf.at[u, 1 - c]
        held[...] = pbuf[u, c]

        @pl.when(z > 0)
        def _():
            arrived(zrecv.at[z, b], zr_sem.at[z, b])
            held[...] += zrecv[z, b].astype(F32)

        @pl.when(z < 3)
        def _():
            arrived(zrecv.at[4, b], zr_sem.at[4, b])
            held[...] += zrecv[4, b].astype(F32)

        hbuf[b] = held[...].astype(BF16)
        place = pl.ds(pl.multiple_of(c * HALF + 128 * b, 128), 128)
        copy = pltpu.make_async_copy(hbuf.at[b], hand_hbm.at[place], hl_sem.at[b])
        copy.start()
        locals_.append(copy)
        send(hbuf.at[b], hand_hbm.at[place], h_sem.at[0, b], h_sem.at[1, b], at(1 - c))
        hidden = hbuf[b].astype(F32)
        sq1[b // 2, x, b % 2] = lax.dot_general(
            jnp.ones((8, COLS), F32), hidden * hidden, (((1,), (1,)), ((), ())),
            precision=lax.Precision.HIGHEST, preferred_element_type=F32,
        )

    met_key_weights = []

    def keys_1(g):
        if not met_key_weights:
            met_key_weights.append(g)
            await_key_weights()
        partial = jnp.zeros((GROUP, KEYS), F32)
        for k in range(4):
            u = UNITS.index((k, 2 * g))
            assert UNITS[u + 1] == (k, 2 * g + 1)
            held = jnp.concatenate([pbuf[u, c], pbuf[u + 1, c]], axis=0).astype(BF16)
            partial += dot(held, gkb[owner[k]].reshape(COLS, KEYS))
        k1s[g] = partial.astype(BF16)
        for d in range(1, 4):
            to = plus(x, 4 - d)
            send(k1s.at[g, pl.ds(pl.multiple_of(to * 64, 64), 64)], k1r.at[g, d],
                 ks_sem.at[0, g, d], kr_sem.at[0, g, d], at(x_=to))

    def keys_2(g):
        total = k1s[g, pl.ds(pl.multiple_of(x * 64, 64), 64), :].astype(F32)
        for d in range(1, 4):
            arrived(k1r.at[g, d], kr_sem.at[0, g, d])
            total += k1r[g, d].astype(F32)
        k2s[g] = total.astype(BF16)
        for e in range(1, 4):
            to = plus(z, e)
            send(k2s.at[g, pl.ds(pl.multiple_of(to * 16, 16), 16)], k2r.at[g, e],
                 ks_sem.at[1, g, e], kr_sem.at[1, g, e], at(z_=to))

    def keys_3(g):
        mine_ = pl.ds(pl.multiple_of(z * 16, 16), 16)
        total = k2s[g, mine_, :].astype(F32)
        for e in range(1, 4):
            arrived(k2r.at[g, e], kr_sem.at[1, g, e])
            total += k2r[g, e].astype(F32)
        place = pl.ds(pl.multiple_of(x * 64 + z * 16, 16), 16)
        k3[g, place, :] = total.astype(BF16)
        for e in range(1, 4):
            send(k3.at[g, place], k3.at[g, place], ks_sem.at[2, g, e], kr_sem.at[2, g, e],
                 at(z_=plus(z, e)))

    def keys_4(g):
        for e in range(1, 4):
            place = pl.ds(pl.multiple_of(x * 64 + plus(z, 4 - e) * 16, 16), 16)
            arrived(k3.at[g, place], kr_sem.at[2, g, e])
        held = k3.at[g, pl.ds(pl.multiple_of(x * 64, 64), 64)]
        place = keys_hbm.at[pl.ds(pl.multiple_of(GROUP * g + x * 64, 64), 64)]
        copy = pltpu.make_async_copy(held, place, kl_sem.at[g])
        copy.start()
        locals_.append(copy)
        for d in range(1, 4):
            send(held, place, ks_sem.at[3, g, d], kr_sem.at[3, g, d], at(x_=plus(x, d)))

    def squares_1(g):
        for d in range(1, 4):
            send(sq1.at[g, x], sq1.at[g, x], qs_sem.at[0, g, d], qr_sem.at[0, g, d],
                 at(x_=plus(x, d)))

    def squares_2(g):
        for d in range(1, 4):
            arrived(sq1.at[g, plus(x, 4 - d)], qr_sem.at[0, g, d])
        sq2[g, z] = (sq1[g, 0] + sq1[g, 1]) + (sq1[g, 2] + sq1[g, 3])
        for e in range(1, 4):
            send(sq2.at[g, z], sq2.at[g, z], qs_sem.at[1, g, e], qr_sem.at[1, g, e],
                 at(z_=plus(z, e)))

    def keys_5(g):
        for d in range(1, 4):
            place = pl.ds(pl.multiple_of(GROUP * g + plus(x, 4 - d) * 64, 64), 64)
            arrived(keys_hbm.at[place], kr_sem.at[3, g, d])
        for e in range(1, 4):
            arrived(sq2.at[g, plus(z, 4 - e)], qr_sem.at[1, g, e])
        squares_ref[g] = (sq2[g, 0] + sq2[g, 1]) + (sq2[g, 2] + sq2[g, 3])

    local_res.wait()
    send_weights(0)
    send_weights(1)
    send_weights(2)
    send_key_weights(0)
    share_weights(0)
    share_weights(1)
    pass_pair(0)
    await_pair(0)
    context_block(3)
    pass_weights(0)
    share_weights(2)
    share_weights(3)
    context_block(1)
    pass_context(3)
    pass_weights(1)
    share_weights(5)
    context_block(2)
    pass_context(1)
    share_weights(4)
    pass_weights(3)
    multiply(3)
    pass_weights(2)
    share_key_weights(0)
    add_half(3)
    pass_weights(5)
    pass_context(2)
    pass_on(3)
    send_weights(3)
    multiply(1)
    context_block(0)
    multiply(2)
    add_half(1)
    pass_on(1)
    multiply(7)
    multiply(5)
    pass_weights(4)
    multiply(6)
    share_weights(6)
    share_weights(7)
    add_half(2)
    pass_on(2)
    pass_key_weights(0)
    add_half(7)
    add_half(5)
    pass_context(0)
    pass_on(7)
    add_half(6)
    multiply(11)
    multiply(10)
    multiply(9)
    pass_on(5)
    pass_weights(6)
    add_half(11)
    multiply(8)
    multiply(0)
    add_half(9)
    multiply(4)
    pass_weights(7)
    add_half(10)
    add_half(8)
    add_half(0)
    pass_on(0)
    swap_key_weights(0)
    pass_on(6)
    pass_on(11)
    multiply(14)
    multiply(15)
    multiply(13)
    pass_on(10)
    multiply(12)
    add_half(14)
    add_half(15)
    keys_1(1)
    add_half(4)
    pass_on(9)
    add_half(13)
    add_half(12)
    keys_1(0)
    hand(3)
    keys_2(1)
    pass_on(4)
    hand(2)
    keys_2(0)
    squares_1(1)
    keys_3(1)
    pass_on(8)
    hand(1)
    keys_3(0)
    squares_2(1)
    keys_4(1)
    hand(0)
    squares_1(0)
    keys_4(0)
    keys_5(1)
    squares_2(0)
    keys_5(0)
    for b in range(4):
        place = pl.ds(pl.multiple_of((1 - c) * HALF + 128 * b, 128), 128)
        arrived(hand_hbm.at[place], h_sem.at[1, b])
    for copy in locals_:
        copy.wait()
    for copy in started:
        copy.wait_send()


def rotation():
    angles = np.arange(LEN)[:, None] * THETA ** (-2.0 * np.arange(HEAD // 2) / HEAD)[None, :]
    cosine, sine = np.cos(angles), np.sin(angles)
    return np.stack(
        [np.concatenate([cosine, cosine], 1), np.concatenate([-sine, sine], 1)]
    ).astype(np.float32)


def deliver(hand_in, keys_in, squares_ref, bias_ref, rot_hbm, hand_out, keys_out, hand, keys, out, rot, sem):
    rows = [pl.ds(256 * i, 256) for i in range(4)]
    half = pl.ds(pl.multiple_of(lax.axis_index("section") * HALF, HALF), HALF)
    first = [pltpu.make_async_copy(hand_in.at[r], hand.at[r], sem.at[0, i]) for i, r in enumerate(rows)]
    second = [pltpu.make_async_copy(hand.at[r], hand_out.at[r], sem.at[1, i]) for i, r in enumerate(rows)]
    keys_first = [pltpu.make_async_copy(keys_in.at[r], keys.at[r], sem.at[0, 4 + i]) for i, r in enumerate(rows[:2])]
    keys_second = [pltpu.make_async_copy(out.at[r], keys_out.at[r], sem.at[1, 4 + i]) for i, r in enumerate(rows[:2])]
    angles = pltpu.make_async_copy(rot_hbm.at[:, half], rot, sem.at[0, 6])
    for copy in [*first, *keys_first, angles]:
        copy.start()
    for arriving, leaving in zip(first, second, strict=True):
        arriving.wait()
        leaving.start()
    inverse = lax.rsqrt(squares_ref[...] / D + EPS)
    angles.wait()
    for g in range(2):
        keys_first[g].wait()
        for i in range(2):
            at_rows = pl.ds(GROUP * g + 128 * i, 128)
            projected = keys[at_rows, :].astype(F32) * inverse[g, i].T[:, :1] + bias_ref[...]
            cosine, sine = rot[0, at_rows, :], rot[1, at_rows, :]
            for head in range(KEYS // HEAD):
                v = projected[:, head * HEAD : (head + 1) * HEAD]
                crossed = jnp.concatenate([v[:, HEAD // 2 :], v[:, : HEAD // 2]], axis=1)
                out[at_rows, pl.ds(head * HEAD, HEAD)] = (v * cosine + crossed * sine).astype(BF16)
        keys_second[g].start()
    for copy in second + keys_second:
        copy.wait()


def local(queries, keys_values, segments, residual, out_weight, key_weight, key_bias, norm_gain):
    hbm = pl.BlockSpec(memory_space=pl.ANY)
    vmem = pl.BlockSpec(memory_space=pltpu.VMEM)
    dma = pltpu.SemaphoreType.DMA
    handed, keys, squares = pl.pallas_call(
        kernel,
        out_shape=(
            jax.ShapeDtypeStruct((LEN, COLS), BF16),
            jax.ShapeDtypeStruct((HALF, KEYS), BF16),
            jax.ShapeDtypeStruct((2, 2, 8, 128), F32),
        ),
        in_specs=[hbm, hbm, vmem, hbm, hbm, hbm, vmem],
        out_specs=(hbm, hbm, vmem),
        scratch_shapes=[
            pltpu.VMEM((LEN, 256), BF16),
            pltpu.VMEM((2, LEN, HEAD), BF16),
            pltpu.VMEM((4, 4, 256, COLS), BF16),
            pltpu.VMEM((HALF, COLS), BF16),
            pltpu.VMEM((COLS, KEYS), BF16),
            pltpu.VMEM((4, 2, 256, KEYS), BF16),
            pltpu.VMEM((4, 4, 256, 256), BF16),
            pltpu.VMEM((16, 2, 128, COLS), F32),
            pltpu.VMEM((16, 128, COLS), BF16),
            pltpu.VMEM((16, 128, COLS), BF16),
            pltpu.VMEM((3, 4, 128, COLS), BF16),
            pltpu.VMEM((5, 4, 128, COLS), BF16),
            pltpu.VMEM((4, 128, COLS), BF16),
            pltpu.VMEM((2, GROUP, KEYS), BF16),
            pltpu.VMEM((2, 4, 64, KEYS), BF16),
            pltpu.VMEM((2, 64, KEYS), BF16),
            pltpu.VMEM((2, 4, 16, KEYS), BF16),
            pltpu.VMEM((2, GROUP, KEYS), BF16),
            pltpu.VMEM((2, 4, 2, 8, 128), F32),
            pltpu.VMEM((2, 4, 2, 8, 128), F32),
            dma((6,)),
            dma((4,)),
            dma((4,)),
            dma((2, 4, 4)),
            dma((2, 8, 4)),
            dma((2, 4, 4)),
            dma((2, 16)),
            dma((3, 4)),
            dma((5, 4)),
            dma((2, 4)),
            dma((4,)),
            dma((5, 4)),
            dma((5, 4)),
            dma((4, 2, 4)),
            dma((4, 2, 4)),
            dma((2,)),
            dma((2, 2, 4)),
            dma((2, 2, 4)),
        ],
        compiler_params=pltpu.CompilerParams(
            collective_id=0, has_side_effects=True, vmem_limit_bytes=56 << 20
        ),
        name="relay",
    )(
        queries[0], keys_values[0], segments, residual[0], out_weight, key_weight,
        norm_gain.reshape(1, COLS),
    )
    handed, keys = pl.pallas_call(
        deliver,
        out_shape=(
            jax.ShapeDtypeStruct((LEN, COLS), BF16),
            jax.ShapeDtypeStruct((HALF, KEYS), BF16),
        ),
        in_specs=[hbm, hbm, vmem, vmem, hbm],
        out_specs=(hbm, hbm),
        scratch_shapes=[
            pltpu.VMEM((LEN, COLS), BF16),
            pltpu.VMEM((HALF, KEYS), BF16),
            pltpu.VMEM((HALF, KEYS), BF16),
            pltpu.VMEM((2, HALF, HEAD), F32),
            dma((2, 7)),
        ],
        compiler_params=pltpu.CompilerParams(vmem_limit_bytes=60 << 20),
        name="deliver",
    )(handed, keys, squares, key_bias.reshape(1, KEYS), jnp.asarray(rotation()))
    return handed[None], keys[None]


def solution(mesh):
    return jax.shard_map(
        local,
        mesh=mesh,
        in_specs=(
            P("narrow", None, "wide"),
            P("narrow", None, "wide"),
            P("narrow", None),
            P("narrow", None, "wide"),
            P("wide", None),
            P("wide", None),
            P(),
            P("wide"),
        ),
        out_specs=(P("narrow", None, "wide"), P("narrow", "section", None)),
        check_vma=False,
    )
```

time: 99.5 us -> 89 us (0.89)
  Pallas kernels: 94.2 us -> 87.8 us
  local copies, waits for them, and re-layouts: 4.13 us -> 0 us
    pallas_call x1, Pallas kernels: 94.2 us -> 83.8 us  [local(): pl.pallas_call(kernel, out_shape=(jax.ShapeDtypeStruct((LEN, COLS), BF16)...]
    unnamed x2 -> x0, local copies, waits for them, and re-layouts: 4.13 us -> none
    pallas_call x0 -> x1, Pallas kernels: none -> 4 us  [local(): pl.pallas_call(deliver, out_shape=(jax.ShapeDtypeStruct((LEN, COLS), BF16...]
where the time goes in v2:
time: 89 us; the launch traced here: 88.4 us
  Pallas kernels  87.8 us (99%)
    pallas_call x1, Pallas kernels, local(): pl.pallas_call(kernel, out_shape=(jax.ShapeDtypeStruct((LEN, COLS), BF16)...  83.8 us
    pallas_call x1, Pallas kernels, local(): pl.pallas_call(deliver, out_shape=(jax.ShapeDtypeStruct((LEN, COLS), BF16...  4 us

profile of v2, /device:TPU:8, one launch (start us, length us, event | category | flops | bytes accessed | tf_op | source)
XLA Modules:
  0.0 88.4 jit_solution(8467671428672702298)
XLA Ops:
  0.6 83.8 %relay.1 = (bf16[1024,512]{1,0:T(8,128)(2,1)}, bf16[512,512]{1,0:T(8,128)(2,1)}, f32[2,2,8,128]{3,2,1,0:T(8,128)}) custom-call(bf16[1024,512]{1,0:T(8,128)(2,1)} %bitcast.7, bf16[1024,128]{1,0:T(8,128)(2,1)} %bitcast.9, s32[1,1024]{1,0:T(1,128)} %seg_ref.1, bf16[1024,512]{1,0:T(8,128)(2,1)} %bitcast.8, bf16[512,8192]{1,0:T(8,128)(2,1)} %w_hbm.1, ...), custom_call_target="tpu_custom_call" | custom-call | tf_op jit(solution)/shard_map/relay/pallas_call | solution.py:514
  84.4 4.0 %deliver.1 = (bf16[1024,512]{1,0:T(8,128)(2,1)}, bf16[512,512]{1,0:T(8,128)(2,1)}) custom-call(bf16[1024,512]{1,0:T(8,128)(2,1)} %get-tuple-element.7.hand_in, bf16[512,512]{1,0:T(8,128)(2,1)} %get-tuple-element.8.keys_in, f32[2,2,8,128]{3,2,1,0:T(8,128)} %get-tuple-element.9.squares_ref, f32[1,512]{1,0:T(1,128)} %bitcast.10, ...), custom_call_target="tpu_custom_call" | custom-call | tf_op jit(solution)/shard_map/deliver/pallas_call | solution.py:571

commit v3 on v2

--- a/solution.py
+++ b/solution.py
@@ -477,7 +477,10 @@
     ).astype(np.float32)
 
 
-def deliver(hand_in, keys_in, squares_ref, bias_ref, rot_hbm, hand_out, keys_out, hand, keys, out, rot, sem):
+def deliver(
+    hand_in, keys_in, squares_hbm, bias_hbm, rot_hbm, hand_out, keys_out,
+    hand, keys, out, rot, squares_ref, bias_ref, sem,
+):
     rows = [pl.ds(256 * i, 256) for i in range(4)]
     half = pl.ds(pl.multiple_of(lax.axis_index("section") * HALF, HALF), HALF)
     first = [pltpu.make_async_copy(hand_in.at[r], hand.at[r], sem.at[0, i]) for i, r in enumerate(rows)]
@@ -485,11 +488,17 @@
     keys_first = [pltpu.make_async_copy(keys_in.at[r], keys.at[r], sem.at[0, 4 + i]) for i, r in enumerate(rows[:2])]
     keys_second = [pltpu.make_async_copy(out.at[r], keys_out.at[r], sem.at[1, 4 + i]) for i, r in enumerate(rows[:2])]
     angles = pltpu.make_async_copy(rot_hbm.at[:, half], rot, sem.at[0, 6])
-    for copy in [*first, *keys_first, angles]:
+    small = [
+        pltpu.make_async_copy(squares_hbm, squares_ref, sem.at[0, 7]),
+        pltpu.make_async_copy(bias_hbm, bias_ref, sem.at[0, 8]),
+    ]
+    for copy in [*first, *small, *keys_first, angles]:
         copy.start()
     for arriving, leaving in zip(first, second, strict=True):
         arriving.wait()
         leaving.start()
+    for copy in small:
+        copy.wait()
     inverse = lax.rsqrt(squares_ref[...] / D + EPS)
     angles.wait()
     for g in range(2):
@@ -574,14 +583,16 @@
             jax.ShapeDtypeStruct((LEN, COLS), BF16),
             jax.ShapeDtypeStruct((HALF, KEYS), BF16),
         ),
-        in_specs=[hbm, hbm, vmem, vmem, hbm],
+        in_specs=[hbm, hbm, hbm, hbm, hbm],
         out_specs=(hbm, hbm),
         scratch_shapes=[
             pltpu.VMEM((LEN, COLS), BF16),
             pltpu.VMEM((HALF, KEYS), BF16),
             pltpu.VMEM((HALF, KEYS), BF16),
             pltpu.VMEM((2, HALF, HEAD), F32),
-            dma((2, 7)),
+            pltpu.VMEM((2, 2, 8, 128), F32),
+            pltpu.VMEM((1, KEYS), F32),
+            dma((2, 9)),
         ],
         compiler_params=pltpu.CompilerParams(vmem_limit_bytes=60 << 20),
         name="deliver",

time: 89 us -> 88.3 us (level)
  no operation moved by 1% of the time
where the time goes in v3:
time: 88.3 us; the launch traced here: 87.7 us
  Pallas kernels  87.1 us (99%)
    pallas_call x1, Pallas kernels, local(): pl.pallas_call(kernel, out_shape=(jax.ShapeDtypeStruct((LEN, COLS), BF16)...  83.8 us
    pallas_call x1, Pallas kernels, local(): pl.pallas_call(deliver, out_shape=(jax.ShapeDtypeStruct((LEN, COLS), BF16...  3.35 us

profile of v3, /device:TPU:8, one launch (start us, length us, event | category | flops | bytes accessed | tf_op | source)
XLA Modules:
  0.0 87.7 jit_solution(4169855612886802492)
XLA Ops:
  0.6 83.8 %relay.1 = (bf16[1024,512]{1,0:T(8,128)(2,1)}, bf16[512,512]{1,0:T(8,128)(2,1)}, f32[2,2,8,128]{3,2,1,0:T(8,128)}) custom-call(bf16[1024,512]{1,0:T(8,128)(2,1)} %bitcast.7, bf16[1024,128]{1,0:T(8,128)(2,1)} %bitcast.9, s32[1,1024]{1,0:T(1,128)} %seg_ref.1, bf16[1024,512]{1,0:T(8,128)(2,1)} %bitcast.8, bf16[512,8192]{1,0:T(8,128)(2,1)} %w_hbm.1, ...), custom_call_target="tpu_custom_call" | custom-call | tf_op jit(solution)/shard_map/relay/pallas_call | solution.py:523
  84.4 3.4 %deliver.1 = (bf16[1024,512]{1,0:T(8,128)(2,1)}, bf16[512,512]{1,0:T(8,128)(2,1)}) custom-call(bf16[1024,512]{1,0:T(8,128)(2,1)} %get-tuple-element.7.hand_in, bf16[512,512]{1,0:T(8,128)(2,1)} %get-tuple-element.8.keys_in, f32[2,2,8,128]{3,2,1,0:T(8,128)} %get-tuple-element.9.squares_hbm, f32[1,512]{1,0:T(1,128)} %bitcast.10, ...), custom_call_target="tpu_custom_call" | custom-call | tf_op jit(solution)/shard_map/deliver/pallas_call | solution.py:580

commit v4 on v3

--- a/solution.py
+++ b/solution.py
@@ -372,94 +372,94 @@
     share_weights(1)
     pass_pair(0)
     await_pair(0)
-    context_block(3)
+    context_block(0)
     pass_weights(0)
     share_weights(2)
     share_weights(3)
-    context_block(1)
-    pass_context(3)
+    context_block(2)
+    pass_context(0)
     pass_weights(1)
     share_weights(5)
-    context_block(2)
-    pass_context(1)
+    context_block(1)
+    pass_context(2)
     share_weights(4)
     pass_weights(3)
-    multiply(3)
+    multiply(0)
     pass_weights(2)
     share_key_weights(0)
-    add_half(3)
+    add_half(0)
     pass_weights(5)
-    pass_context(2)
-    pass_on(3)
+    pass_context(1)
+    pass_on(0)
     send_weights(3)
+    multiply(2)
+    context_block(3)
     multiply(1)
-    context_block(0)
-    multiply(2)
+    add_half(2)
+    pass_on(2)
+    multiply(4)
+    multiply(6)
+    pass_weights(4)
+    multiply(5)
+    share_weights(6)
+    share_weights(7)
     add_half(1)
     pass_on(1)
+    pass_key_weights(0)
+    add_half(4)
+    add_half(6)
+    pass_context(3)
+    pass_on(4)
+    add_half(5)
+    multiply(8)
+    multiply(9)
+    multiply(10)
+    pass_on(6)
+    pass_weights(6)
+    add_half(8)
+    multiply(11)
+    multiply(3)
+    add_half(10)
     multiply(7)
-    multiply(5)
-    pass_weights(4)
-    multiply(6)
-    share_weights(6)
-    share_weights(7)
-    add_half(2)
-    pass_on(2)
-    pass_key_weights(0)
+    pass_weights(7)
+    add_half(9)
+    add_half(11)
+    add_half(3)
+    pass_on(3)
+    swap_key_weights(0)
+    pass_on(5)
+    pass_on(8)
+    multiply(13)
+    multiply(12)
+    multiply(14)
+    pass_on(9)
+    multiply(15)
+    add_half(13)
+    add_half(12)
+    keys_1(0)
     add_half(7)
-    add_half(5)
-    pass_context(0)
-    pass_on(7)
-    add_half(6)
-    multiply(11)
-    multiply(10)
-    multiply(9)
-    pass_on(5)
-    pass_weights(6)
-    add_half(11)
-    multiply(8)
-    multiply(0)
-    add_half(9)
-    multiply(4)
-    pass_weights(7)
-    add_half(10)
-    add_half(8)
-    add_half(0)
-    pass_on(0)
-    swap_key_weights(0)
-    pass_on(6)
-    pass_on(11)
-    multiply(14)
-    multiply(15)
-    multiply(13)
     pass_on(10)
-    multiply(12)
     add_half(14)
     add_half(15)
     keys_1(1)
-    add_half(4)
-    pass_on(9)
-    add_half(13)
-    add_half(12)
-    keys_1(0)
+    hand(0)
+    keys_2(0)
+    pass_on(7)
+    hand(1)
+    keys_2(1)
+    squares_1(0)
+    keys_3(0)
+    pass_on(11)
+    hand(2)
+    keys_3(1)
+    squares_2(0)
+    keys_4(0)
     hand(3)
-    keys_2(1)
-    pass_on(4)
-    hand(2)
-    keys_2(0)
     squares_1(1)
-    keys_3(1)
-    pass_on(8)
-    hand(1)
-    keys_3(0)
+    keys_4(1)
+    keys_5(0)
     squares_2(1)
-    keys_4(1)
-    hand(0)
-    squares_1(0)
-    keys_4(0)
     keys_5(1)
-    squares_2(0)
-    keys_5(0)
     for b in range(4):
         place = pl.ds(pl.multiple_of((1 - c) * HALF + 128 * b, 128), 128)
         arrived(hand_hbm.at[place], h_sem.at[1, b])

time: 88.3 us -> 90.3 us (1.023)
  Pallas kernels: 87.1 us -> 89.3 us
    pallas_call x1, Pallas kernels: 83.8 us -> 86 us  [local(): pl.pallas_call(kernel, out_shape=(jax.ShapeDtypeStruct((LEN, COLS), BF16)...]
where the time goes in v4:
time: 90.3 us; the launch traced here: 90.1 us
  Pallas kernels  89.3 us (99%)
    pallas_call x1, Pallas kernels, local(): pl.pallas_call(kernel, out_shape=(jax.ShapeDtypeStruct((LEN, COLS), BF16)...  86 us
    pallas_call x1, Pallas kernels, local(): pl.pallas_call(deliver, out_shape=(jax.ShapeDtypeStruct((LEN, COLS), BF16...  3.35 us

profile of v4, /device:TPU:8, one launch (start us, length us, event | category | flops | bytes accessed | tf_op | source)
XLA Modules:
  0.0 90.1 jit_solution(17179400025347339559)
XLA Ops:
  0.6 86.0 %relay.1 = (bf16[1024,512]{1,0:T(8,128)(2,1)}, bf16[512,512]{1,0:T(8,128)(2,1)}, f32[2,2,8,128]{3,2,1,0:T(8,128)}) custom-call(bf16[1024,512]{1,0:T(8,128)(2,1)} %bitcast.7, bf16[1024,128]{1,0:T(8,128)(2,1)} %bitcast.9, s32[1,1024]{1,0:T(1,128)} %seg_ref.1, bf16[1024,512]{1,0:T(8,128)(2,1)} %bitcast.8, bf16[512,8192]{1,0:T(8,128)(2,1)} %w_hbm.1, ...), custom_call_target="tpu_custom_call" | custom-call | tf_op jit(solution)/shard_map/relay/pallas_call | solution.py:523
  86.6 3.4 %deliver.1 = (bf16[1024,512]{1,0:T(8,128)(2,1)}, bf16[512,512]{1,0:T(8,128)(2,1)}) custom-call(bf16[1024,512]{1,0:T(8,128)(2,1)} %get-tuple-element.7.hand_in, bf16[512,512]{1,0:T(8,128)(2,1)} %get-tuple-element.8.keys_in, f32[2,2,8,128]{3,2,1,0:T(8,128)} %get-tuple-element.9.squares_hbm, f32[1,512]{1,0:T(1,128)} %bitcast.10, ...), custom_call_target="tpu_custom_call" | custom-call | tf_op jit(solution)/shard_map/deliver/pallas_call | solution.py:580
